TPU v7x, 256 devices: a whole 4x4x8 slice. The times are simulated.
256 devices in a mesh: section: 16 (over z, x_hi), dp: 16 (over x_lo, y, core).
Axes of the slice: x: 4 (x_hi: 2, x_lo: 2; x = x_hi * 2 + x_lo), y: 4, z: 8, core: 2. Of those that a mesh axis runs over, the one named last changes fastest.
Arguments:
- saved_a: bfloat16 [16, 2, 512, 5120], P('section', None, 'dp'), may hold values from -8 to 8
- saved_b: bfloat16 [16, 2, 512, 5120], P('section', None, 'dp'), may hold values from -8 to 8
- cot_a: bfloat16 [2, 512, 5120], P(None, 'dp'), may hold values from -0.125 to 0.125
- cot_b: bfloat16 [2, 512, 5120], P(None, 'dp'), may hold values from -0.125 to 0.125
- w_in: bfloat16 [16, 2, 5120, 256], P('section', None, 'dp'), may hold values from -0.01953125 to 0.01953125
- w_out: bfloat16 [16, 2, 256, 5120], P('section', None, 'dp'), may hold values from -0.078125 to 0.078125
- decay_rate: float32 [16, 2, 256], P('section'), may hold values from 0.004 to 0.4
Outputs:
- grad_w_in: float32 [16, 2, 5120, 256], P('section', None, 'dp')
- grad_w_out: float32 [16, 2, 256, 5120], P('section', None, 'dp')
All inputs are finite; a program needn't handle non-finite values.
Results may differ from a plain program's by a relative error of at most 0.025.
Values may be sent and summed in bfloat16 or wider, within the bound.
No kernel may reach another device: no remote copies, remote signals or barrier semaphores. Data moves between devices by JAX's collectives and lax.ppermute only.
A program may use at most 64 MiB of HBM per device.

v0:
```python
import jax
import jax.numpy as jnp
from jax import lax
from jax.sharding import PartitionSpec as P


def passed_along(block, axis, distance):
    devices = range(lax.axis_size(axis))
    route = [(i - distance, i) for i in devices if i - distance in devices]
    return lax.ppermute(block, axis, route)


def decay_powers(rates, length, flipped):
    places = jnp.arange(length)
    distance = places[:, None] - places[None, :]
    if flipped:
        distance = -distance
    reach = jnp.maximum(distance, 0).astype(jnp.float32)
    powers = jnp.exp(-reach[:, :, None] * rates[None, None, :])
    return jnp.where((distance >= 0)[:, :, None], powers, 0.0)


def recompute_states(inputs, w_input, powers):
    hidden = lax.dot_general(
        inputs, w_input, (((2,), (0,)), ((), ())), preferred_element_type=jnp.float32
    )
    return jnp.einsum("tuc,muc->mtc", powers, hidden).astype(jnp.bfloat16)


def block_backward(upstream, w_input, w_output, powers):
    latent_grad = lax.dot_general(
        upstream, w_output, (((1,), (1,)), ((), ())), preferred_element_type=jnp.float32
    )
    state_grad = jnp.einsum("tuc,uc->tc", powers, latent_grad).astype(jnp.bfloat16)
    carried = lax.dot_general(
        state_grad, w_input, (((1,), (1,)), ((), ())), preferred_element_type=jnp.float32
    )
    return (state_grad, (upstream.astype(jnp.float32) + carried).astype(jnp.bfloat16))


def record(store, value, slot, valid):
    previous = lax.dynamic_index_in_dim(store, slot, 0, keepdims=False)
    return lax.dynamic_update_index_in_dim(store, jnp.where(valid, value, previous), slot, 0)


def weight_terms(inputs, latent, upstream_all, state_all):
    grad_input = lax.dot_general(
        inputs, state_all, (((0, 1), (0, 1)), ((), ())), preferred_element_type=jnp.float32
    )
    grad_output = lax.dot_general(
        latent, upstream_all, (((0, 1), (0, 1)), ((), ())), preferred_element_type=jnp.float32
    )
    return (grad_input, grad_output)


def on_device(saved_a, saved_b, cot_a, cot_b, w_in, w_out, decay_rate):
    sections = lax.axis_size("section")
    position = lax.axis_index("section")
    inputs_down = saved_a[0]
    inputs_up = saved_b[0]
    micro = inputs_down.shape[0]
    length = inputs_down.shape[1]
    width = inputs_down.shape[2]
    weights_in, weights_out = (
        lax.all_gather(w_in[0], "dp", axis=1, tiled=True),
        lax.all_gather(w_out[0], "dp", axis=1, tiled=True),
    )
    state_width = weights_in.shape[2]
    ahead_down = decay_powers(decay_rate[0, 0], length, False)
    behind_down = decay_powers(decay_rate[0, 0], length, True)
    ahead_up = decay_powers(decay_rate[0, 1], length, False)
    behind_up = decay_powers(decay_rate[0, 1], length, True)
    latent_down = recompute_states(inputs_down, weights_in[0], ahead_down)
    latent_up = recompute_states(inputs_up, weights_in[1], ahead_up)

    def advance(moment, carry):
        incoming_down, incoming_up, upper_down, state_down, upper_up, state_up = carry
        order_down = moment - (sections - 1 - position)
        valid_down = (order_down >= 0) & (order_down < micro)
        slot_down = jnp.clip(order_down, 0, micro - 1)
        arriving_down = lax.dynamic_index_in_dim(cot_a, slot_down, 0, keepdims=False)
        upstream_down = jnp.where(position == sections - 1, arriving_down, incoming_down)
        grad_state_down, passing_down = block_backward(
            upstream_down, weights_in[0], weights_out[0], behind_down
        )
        upper_down = record(upper_down, upstream_down, slot_down, valid_down)
        state_down = record(state_down, grad_state_down, slot_down, valid_down)
        order_up = moment - position
        valid_up = (order_up >= 0) & (order_up < micro)
        slot_up = jnp.clip(order_up, 0, micro - 1)
        arriving_up = lax.dynamic_index_in_dim(cot_b, slot_up, 0, keepdims=False)
        upstream_up = jnp.where(position == 0, arriving_up, incoming_up)
        grad_state_up, passing_up = block_backward(
            upstream_up, weights_in[1], weights_out[1], behind_up
        )
        upper_up = record(upper_up, upstream_up, slot_up, valid_up)
        state_up = record(state_up, grad_state_up, slot_up, valid_up)
        incoming_down = passed_along(passing_down, "section", -1)
        incoming_up = passed_along(passing_up, "section", 1)
        return (incoming_down, incoming_up, upper_down, state_down, upper_up, state_up)

    empty_rows = jnp.zeros((length, width), jnp.bfloat16)
    empty_upper = jnp.zeros((micro, length, width), jnp.bfloat16)
    empty_state = jnp.zeros((micro, length, state_width), jnp.bfloat16)
    start = (empty_rows, empty_rows, empty_upper, empty_state, empty_upper, empty_state)
    finished = lax.fori_loop(0, micro + sections - 1, advance, start)
    upper_down, state_down, upper_up, state_up = (
        finished[2],
        finished[3],
        finished[4],
        finished[5],
    )
    in_down, out_down = weight_terms(inputs_down, latent_down, upper_down, state_down)
    in_up, out_up = weight_terms(inputs_up, latent_up, upper_up, state_up)
    in_down, out_down, in_up, out_up = (
        lax.psum_scatter(
            in_down.astype(jnp.bfloat16), "dp", scatter_dimension=0, tiled=True
        ).astype(jnp.float32),
        lax.psum_scatter(
            out_down.astype(jnp.bfloat16), "dp", scatter_dimension=0, tiled=True
        ).astype(jnp.float32),
        lax.psum_scatter(in_up.astype(jnp.bfloat16), "dp", scatter_dimension=0, tiled=True).astype(
            jnp.float32
        ),
        lax.psum_scatter(out_up.astype(jnp.bfloat16), "dp", scatter_dimension=0, tiled=True).astype(
            jnp.float32
        ),
    )
    grad_w_in = jnp.stack([in_down, in_up])[None]
    grad_w_out = jnp.stack([out_down, out_up])[None]
    return (grad_w_in, grad_w_out)


def solution(mesh):
    return jax.shard_map(
        on_device,
        mesh=mesh,
        in_specs=(
            P("section", None, "dp", None),
            P("section", None, "dp", None),
            P(None, "dp", None),
            P(None, "dp", None),
            P("section", None, "dp", None),
            P("section", None, "dp", None),
            P("section", None, None),
        ),
        out_specs=(P("section", None, "dp", None), P("section", None, "dp", None)),
        check_vma=False,
    )
```

profile of v0, /device:TPU:4, one launch (start us, length us, event | category | flops | bytes accessed | tf_op | source)
XLA Modules:
  0.0 876.3 jit_solution(721600896775910908)
XLA Ops:
  9.5 44.9 %all-gather.7.cloned.1.call-done = bf16[1,2,5120,256]{3,2,1,0:T(8,128)(2,1)} async-done(((bf16[1,2,320,256]{3,2,1,0:T(8,128)(2,1)}), bf16[1,2,5120,256]{3,2,1,0:T(8,128)(2,1)}) %all-gather.7.cloned.1.call-update) | async-done | bytes 5242896 | tf_op jit(solution)/shard_map/all_gather | solution.py:65
  54.4 44.0 %all-gather.5.cloned.1.call-done = bf16[1,2,256,5120]{3,2,1,0:T(8,128)(2,1)} async-done(((bf16[1,2,16,5120]{3,2,1,0:T(8,128)(2,1)}), bf16[1,2,256,5120]{3,2,1,0:T(8,128)(2,1)}) %all-gather.5.cloned.1.call-update) | async-done | bytes 5242896 | tf_op jit(solution)/shard_map/all_gather | solution.py:66
  98.6 470.7 %while.26 = (s32[]{:T(128)}, bf16[32,5120]{1,0:T(8,128)(2,1)S(1)}, bf16[32,5120]{1,0:T(8,128)(2,1)S(1)}, bf16[2,32,5120]{2,1,0:T(8,128)(2,1)S(1)}, bf16[2,32,256...) while((s32[]{:T(128)}, bf16[32,5120]{1,0:T(8,128)(2,1)S(1)}, ...), condition=%wide.region_1.2_spmd.clone.clone, body=%wide.region_0.1_spmd.clone.clone.sunk | while | flops 339279872 | bytes 61971936 | solution.py:106
  105.5 3.7 collective-permute-start.1
  110.1 3.6 collective-permute-start
  113.8 12.0 %collective-permute-done.1 = bf16[32,5120]{1,0:T(8,128)(2,1)S(1)} collective-permute-done((bf16[32,5120]{1,0:T(8,128)(2,1)S(1)}, bf16[32,5120]{1,0:T(8,128)(2,1)S(1)}, u32[]{:S(2)}, u32[]{:S(2)}) %collective-permute-start.1) | collective-permute-done | bytes 327712 | tf_op jit(solution)/shard_map/while/body/eval_jaxpr/ppermute | solution.py:10
  132.6 4.7 collective-permute-start.1
  140.9 11.1 %collective-permute-done.1 = bf16[32,5120]{1,0:T(8,128)(2,1)S(1)} collective-permute-done((bf16[32,5120]{1,0:T(8,128)(2,1)S(1)}, bf16[32,5120]{1,0:T(8,128)(2,1)S(1)}, u32[]{:S(2)}, u32[]{:S(2)}) %collective-permute-start.1) | collective-permute-done | bytes 327712 | tf_op jit(solution)/shard_map/while/body/eval_jaxpr/ppermute | solution.py:10
  158.9 6.2 collective-permute-start.1
  168.0 4.3 collective-permute-done.1
  172.3 7.3 collective-permute-done
  181.3 2.8 fusion.80
  186.5 6.4 collective-permute-start.1
  195.8 4.3 collective-permute-done.1
  200.1 7.3 collective-permute-done
  209.1 2.8 fusion.80
  214.3 6.4 collective-permute-start.1
  223.6 4.3 collective-permute-done.1
  227.9 7.3 collective-permute-done
  236.9 2.8 fusion.80
  242.2 6.4 collective-permute-start.1
  251.4 4.3 collective-permute-done.1
  255.8 7.3 collective-permute-done
  264.8 2.8 fusion.80
  270.0 6.4 collective-permute-start.1
  279.3 4.3 collective-permute-done.1
  283.6 7.3 collective-permute-done
  292.6 2.8 fusion.80
  297.8 6.4 collective-permute-start.1
  307.1 4.3 collective-permute-done.1
  311.4 7.3 collective-permute-done
  320.4 2.8 fusion.80
  325.7 6.4 collective-permute-start.1
  334.9 4.3 collective-permute-done.1
  339.3 7.3 collective-permute-done
  353.5 6.4 collective-permute-start.1
  362.8 4.3 collective-permute-done.1
  367.1 7.3 collective-permute-done
  381.3 6.4 collective-permute-start.1
  390.6 4.3 collective-permute-done.1
  394.9 7.3 collective-permute-done
  409.1 6.4 collective-permute-start.1
  418.4 4.3 collective-permute-done.1
  422.7 7.3 collective-permute-done
  437.0 6.4 collective-permute-start.1
  446.2 4.3 collective-permute-done.1
  450.5 7.4 collective-permute-done
  464.8 6.4 collective-permute-start.1
  474.1 3.2 collective-permute-done.1
  477.3 7.4 collective-permute-done
  491.6 7.1 collective-permute-start.1
  503.2 8.0 collective-permute-done
  518.0 9.6 %collective-permute-start.1 = (bf16[32,5120]{1,0:T(8,128)(2,1)S(1)}, bf16[32,5120]{1,0:T(8,128)(2,1)S(1)}, u32[]{:S(2)}, u32[]{:S(2)}) collective-permute-start(bf16[32,5120]{1,0:T(8,128)(2,1)S(1)} %fusion.83), channel_id=1, source_target_pairs={{0,16},{16,32},{32,48},{48,64},{64,80},{80,96},{96,112},{112,128},... | collective-permute-start | bytes 983048 | tf_op jit(solution)/shard_map/while/body/eval_jaxpr/ppermute | solution.py:10
  532.2 8.0 collective-permute-done
  547.1 9.6 %collective-permute-start.1 = (bf16[32,5120]{1,0:T(8,128)(2,1)S(1)}, bf16[32,5120]{1,0:T(8,128)(2,1)S(1)}, u32[]{:S(2)}, u32[]{:S(2)}) collective-permute-start(bf16[32,5120]{1,0:T(8,128)(2,1)S(1)} %fusion.83), channel_id=1, source_target_pairs={{0,16},{16,32},{32,48},{48,64},{64,80},{80,96},{96,112},{112,128},... | collective-permute-start | bytes 983048 | tf_op jit(solution)/shard_map/while/body/eval_jaxpr/ppermute | solution.py:10
  561.3 8.0 collective-permute-done
  571.7 4.4 copy.29
  579.6 4.5 copy.31
  584.5 3.9 copy.24
  595.9 3.9 copy.27
  607.0 57.6 %reduce-scatter.13.cloned.1.call-done = bf16[320,256]{1,0:T(8,128)(2,1)} async-done(((bf16[5120,256]{1,0:T(8,128)(2,1)}), bf16[320,256]{1,0:T(8,128)(2,1)}) %reduce-scatter.13.cloned.1.call-update) | async-done | bytes 163856
  665.6 66.6 %reduce-scatter.15.cloned.1.call-done = bf16[320,256]{1,0:T(8,128)(2,1)} async-done(((bf16[5120,256]{1,0:T(8,128)(2,1)}), bf16[320,256]{1,0:T(8,128)(2,1)}) %reduce-scatter.15.cloned.1.call-update) | async-done | bytes 163856
  734.5 65.4 %reduce-scatter.9.cloned.1.call-done = bf16[16,5120]{1,0:T(8,128)(2,1)} async-done(((bf16[256,5120]{1,0:T(8,128)(2,1)}), bf16[16,5120]{1,0:T(8,128)(2,1)}) %reduce-scatter.9.cloned.1.call-update) | async-done | bytes 163856 | tf_op jit(solution)/shard_map/reduce_scatter | solution.py:119
  799.9 67.7 %reduce-scatter.11.cloned.1.call-done = bf16[16,5120]{1,0:T(8,128)(2,1)} async-done(((bf16[256,5120]{1,0:T(8,128)(2,1)}), bf16[16,5120]{1,0:T(8,128)(2,1)}) %reduce-scatter.11.cloned.1.call-update) | async-done | bytes 163856 | tf_op jit(solution)/shard_map/reduce_scatter | solution.py:125
  (317 shorter events, 179.5 us)
Async XLA Ops:
  7.2 562.1 %copy-start = (bf16[1,2,32,5120]{3,2,1,0:T(8,128)(2,1)S(1)}, bf16[1,2,32,5120]{3,2,1,0:T(8,128)(2,1)}, u32[]{:S(2)}) copy-start(bf16[1,2,32,5120]{3,2,1,0:T(8,128)(2,1)} %param.9) | copy-start | bytes 1966084
  7.2 47.2 %all-gather.7.cloned.1.call-start = ((), (), s32[]{:S(2)}) async-start(), calls=%async_computation.7 | async-start | bytes 5570560 | tf_op jit(solution)/shard_map/all_gather | solution.py:65
  7.9 90.5 %all-gather.5.cloned.1.call-start = ((), (), s32[]{:S(2)}) async-start(), calls=%async_computation.6 | async-start | bytes 5570560 | tf_op jit(solution)/shard_map/all_gather | solution.py:66
  8.7 655.9 %reduce-scatter.13.cloned.1.call-start = ((), (), s32[]{:S(2)}) async-start(), calls=%async_computation.8 | async-start | bytes 2785280
  98.6 4.4 copy-start.4
  105.5 20.3 %collective-permute-start.1 = (bf16[32,5120]{1,0:T(8,128)(2,1)S(1)}, bf16[32,5120]{1,0:T(8,128)(2,1)S(1)}, u32[]{:S(2)}, u32[]{:S(2)}) collective-permute-start(bf16[32,5120]{1,0:T(8,128)(2,1)S(1)} %fusion.83), channel_id=1, source_target_pairs={{0,16},{16,32},{32,48},{48,64},{64,80},{80,96},{96,112},{112,128},... | collective-permute-start | bytes 983048 | tf_op jit(solution)/shard_map/while/body/eval_jaxpr/ppermute | solution.py:10
  110.1 15.6 %collective-permute-start = (bf16[32,5120]{1,0:T(8,128)(2,1)S(1)}, bf16[32,5120]{1,0:T(8,128)(2,1)S(1)}, u32[]{:S(2)}, u32[]{:S(2)}) collective-permute-start(bf16[32,5120]{1,0:T(8,128)(2,1)S(1)} %fusion.82), channel_id=1, source_target_pairs={{16,0},{32,16},{48,32},{64,48},{80,64},{96,80},{112,96},{128,112},... | collective-permute-start | bytes 983048 | tf_op jit(solution)/shard_map/while/body/eval_jaxpr/ppermute | solution.py:10
  125.8 4.4 copy-start.4
  132.6 19.5 %collective-permute-start.1 = (bf16[32,5120]{1,0:T(8,128)(2,1)S(1)}, bf16[32,5120]{1,0:T(8,128)(2,1)S(1)}, u32[]{:S(2)}, u32[]{:S(2)}) collective-permute-start(bf16[32,5120]{1,0:T(8,128)(2,1)S(1)} %fusion.83), channel_id=1, source_target_pairs={{0,16},{16,32},{32,48},{48,64},{64,80},{80,96},{96,112},{112,128},... | collective-permute-start | bytes 983048 | tf_op jit(solution)/shard_map/while/body/eval_jaxpr/ppermute | solution.py:10
  138.2 13.9 %collective-permute-start = (bf16[32,5120]{1,0:T(8,128)(2,1)S(1)}, bf16[32,5120]{1,0:T(8,128)(2,1)S(1)}, u32[]{:S(2)}, u32[]{:S(2)}) collective-permute-start(bf16[32,5120]{1,0:T(8,128)(2,1)S(1)} %fusion.82), channel_id=1, source_target_pairs={{16,0},{32,16},{48,32},{64,48},{80,64},{96,80},{112,96},{128,112},... | collective-permute-start | bytes 983048 | tf_op jit(solution)/shard_map/while/body/eval_jaxpr/ppermute | solution.py:10
  152.1 4.4 copy-start.4
  158.9 13.3 %collective-permute-start.1 = (bf16[32,5120]{1,0:T(8,128)(2,1)S(1)}, bf16[32,5120]{1,0:T(8,128)(2,1)S(1)}, u32[]{:S(2)}, u32[]{:S(2)}) collective-permute-start(bf16[32,5120]{1,0:T(8,128)(2,1)S(1)} %fusion.83), channel_id=1, source_target_pairs={{0,16},{16,32},{32,48},{48,64},{64,80},{80,96},{96,112},{112,128},... | collective-permute-start | bytes 983048 | tf_op jit(solution)/shard_map/while/body/eval_jaxpr/ppermute | solution.py:10
  166.0 13.6 %collective-permute-start = (bf16[32,5120]{1,0:T(8,128)(2,1)S(1)}, bf16[32,5120]{1,0:T(8,128)(2,1)S(1)}, u32[]{:S(2)}, u32[]{:S(2)}) collective-permute-start(bf16[32,5120]{1,0:T(8,128)(2,1)S(1)} %fusion.82), channel_id=1, source_target_pairs={{16,0},{32,16},{48,32},{64,48},{80,64},{96,80},{112,96},{128,112},... | collective-permute-start | bytes 983048 | tf_op jit(solution)/shard_map/while/body/eval_jaxpr/ppermute | solution.py:10
  179.7 4.4 copy-start.4
  181.2 4.4 copy-start.1
  186.5 13.6 %collective-permute-start.1 = (bf16[32,5120]{1,0:T(8,128)(2,1)S(1)}, bf16[32,5120]{1,0:T(8,128)(2,1)S(1)}, u32[]{:S(2)}, u32[]{:S(2)}) collective-permute-start(bf16[32,5120]{1,0:T(8,128)(2,1)S(1)} %fusion.83), channel_id=1, source_target_pairs={{0,16},{16,32},{32,48},{48,64},{64,80},{80,96},{96,112},{112,128},... | collective-permute-start | bytes 983048 | tf_op jit(solution)/shard_map/while/body/eval_jaxpr/ppermute | solution.py:10
  193.8 13.7 %collective-permute-start = (bf16[32,5120]{1,0:T(8,128)(2,1)S(1)}, bf16[32,5120]{1,0:T(8,128)(2,1)S(1)}, u32[]{:S(2)}, u32[]{:S(2)}) collective-permute-start(bf16[32,5120]{1,0:T(8,128)(2,1)S(1)} %fusion.82), channel_id=1, source_target_pairs={{16,0},{32,16},{48,32},{64,48},{80,64},{96,80},{112,96},{128,112},... | collective-permute-start | bytes 983048 | tf_op jit(solution)/shard_map/while/body/eval_jaxpr/ppermute | solution.py:10
  207.5 4.4 copy-start.4
  209.1 4.4 copy-start.1
  214.3 13.6 %collective-permute-start.1 = (bf16[32,5120]{1,0:T(8,128)(2,1)S(1)}, bf16[32,5120]{1,0:T(8,128)(2,1)S(1)}, u32[]{:S(2)}, u32[]{:S(2)}) collective-permute-start(bf16[32,5120]{1,0:T(8,128)(2,1)S(1)} %fusion.83), channel_id=1, source_target_pairs={{0,16},{16,32},{32,48},{48,64},{64,80},{80,96},{96,112},{112,128},... | collective-permute-start | bytes 983048 | tf_op jit(solution)/shard_map/while/body/eval_jaxpr/ppermute | solution.py:10
  221.6 13.7 %collective-permute-start = (bf16[32,5120]{1,0:T(8,128)(2,1)S(1)}, bf16[32,5120]{1,0:T(8,128)(2,1)S(1)}, u32[]{:S(2)}, u32[]{:S(2)}) collective-permute-start(bf16[32,5120]{1,0:T(8,128)(2,1)S(1)} %fusion.82), channel_id=1, source_target_pairs={{16,0},{32,16},{48,32},{64,48},{80,64},{96,80},{112,96},{128,112},... | collective-permute-start | bytes 983048 | tf_op jit(solution)/shard_map/while/body/eval_jaxpr/ppermute | solution.py:10
  235.3 4.4 copy-start.4
  236.9 4.4 copy-start.1
  242.2 13.6 %collective-permute-start.1 = (bf16[32,5120]{1,0:T(8,128)(2,1)S(1)}, bf16[32,5120]{1,0:T(8,128)(2,1)S(1)}, u32[]{:S(2)}, u32[]{:S(2)}) collective-permute-start(bf16[32,5120]{1,0:T(8,128)(2,1)S(1)} %fusion.83), channel_id=1, source_target_pairs={{0,16},{16,32},{32,48},{48,64},{64,80},{80,96},{96,112},{112,128},... | collective-permute-start | bytes 983048 | tf_op jit(solution)/shard_map/while/body/eval_jaxpr/ppermute | solution.py:10
  249.5 13.7 %collective-permute-start = (bf16[32,5120]{1,0:T(8,128)(2,1)S(1)}, bf16[32,5120]{1,0:T(8,128)(2,1)S(1)}, u32[]{:S(2)}, u32[]{:S(2)}) collective-permute-start(bf16[32,5120]{1,0:T(8,128)(2,1)S(1)} %fusion.82), channel_id=1, source_target_pairs={{16,0},{32,16},{48,32},{64,48},{80,64},{96,80},{112,96},{128,112},... | collective-permute-start | bytes 983048 | tf_op jit(solution)/shard_map/while/body/eval_jaxpr/ppermute | solution.py:10
  263.1 4.4 copy-start.4
  264.7 4.4 copy-start.1
  270.0 13.6 %collective-permute-start.1 = (bf16[32,5120]{1,0:T(8,128)(2,1)S(1)}, bf16[32,5120]{1,0:T(8,128)(2,1)S(1)}, u32[]{:S(2)}, u32[]{:S(2)}) collective-permute-start(bf16[32,5120]{1,0:T(8,128)(2,1)S(1)} %fusion.83), channel_id=1, source_target_pairs={{0,16},{16,32},{32,48},{48,64},{64,80},{80,96},{96,112},{112,128},... | collective-permute-start | bytes 983048 | tf_op jit(solution)/shard_map/while/body/eval_jaxpr/ppermute | solution.py:10
  277.3 13.7 %collective-permute-start = (bf16[32,5120]{1,0:T(8,128)(2,1)S(1)}, bf16[32,5120]{1,0:T(8,128)(2,1)S(1)}, u32[]{:S(2)}, u32[]{:S(2)}) collective-permute-start(bf16[32,5120]{1,0:T(8,128)(2,1)S(1)} %fusion.82), channel_id=1, source_target_pairs={{16,0},{32,16},{48,32},{64,48},{80,64},{96,80},{112,96},{128,112},... | collective-permute-start | bytes 983048 | tf_op jit(solution)/shard_map/while/body/eval_jaxpr/ppermute | solution.py:10
  291.0 4.4 copy-start.4
  292.6 4.4 copy-start.1
  297.8 13.6 %collective-permute-start.1 = (bf16[32,5120]{1,0:T(8,128)(2,1)S(1)}, bf16[32,5120]{1,0:T(8,128)(2,1)S(1)}, u32[]{:S(2)}, u32[]{:S(2)}) collective-permute-start(bf16[32,5120]{1,0:T(8,128)(2,1)S(1)} %fusion.83), channel_id=1, source_target_pairs={{0,16},{16,32},{32,48},{48,64},{64,80},{80,96},{96,112},{112,128},... | collective-permute-start | bytes 983048 | tf_op jit(solution)/shard_map/while/body/eval_jaxpr/ppermute | solution.py:10
  305.1 13.7 %collective-permute-start = (bf16[32,5120]{1,0:T(8,128)(2,1)S(1)}, bf16[32,5120]{1,0:T(8,128)(2,1)S(1)}, u32[]{:S(2)}, u32[]{:S(2)}) collective-permute-start(bf16[32,5120]{1,0:T(8,128)(2,1)S(1)} %fusion.82), channel_id=1, source_target_pairs={{16,0},{32,16},{48,32},{64,48},{80,64},{96,80},{112,96},{128,112},... | collective-permute-start | bytes 983048 | tf_op jit(solution)/shard_map/while/body/eval_jaxpr/ppermute | solution.py:10
  318.8 4.4 copy-start.4
  320.4 4.4 copy-start.1
  325.7 13.6 %collective-permute-start.1 = (bf16[32,5120]{1,0:T(8,128)(2,1)S(1)}, bf16[32,5120]{1,0:T(8,128)(2,1)S(1)}, u32[]{:S(2)}, u32[]{:S(2)}) collective-permute-start(bf16[32,5120]{1,0:T(8,128)(2,1)S(1)} %fusion.83), channel_id=1, source_target_pairs={{0,16},{16,32},{32,48},{48,64},{64,80},{80,96},{96,112},{112,128},... | collective-permute-start | bytes 983048 | tf_op jit(solution)/shard_map/while/body/eval_jaxpr/ppermute | solution.py:10
  333.0 13.7 %collective-permute-start = (bf16[32,5120]{1,0:T(8,128)(2,1)S(1)}, bf16[32,5120]{1,0:T(8,128)(2,1)S(1)}, u32[]{:S(2)}, u32[]{:S(2)}) collective-permute-start(bf16[32,5120]{1,0:T(8,128)(2,1)S(1)} %fusion.82), channel_id=1, source_target_pairs={{16,0},{32,16},{48,32},{64,48},{80,64},{96,80},{112,96},{128,112},... | collective-permute-start | bytes 983048 | tf_op jit(solution)/shard_map/while/body/eval_jaxpr/ppermute | solution.py:10
  346.6 4.4 copy-start.4
  353.5 13.6 %collective-permute-start.1 = (bf16[32,5120]{1,0:T(8,128)(2,1)S(1)}, bf16[32,5120]{1,0:T(8,128)(2,1)S(1)}, u32[]{:S(2)}, u32[]{:S(2)}) collective-permute-start(bf16[32,5120]{1,0:T(8,128)(2,1)S(1)} %fusion.83), channel_id=1, source_target_pairs={{0,16},{16,32},{32,48},{48,64},{64,80},{80,96},{96,112},{112,128},... | collective-permute-start | bytes 983048 | tf_op jit(solution)/shard_map/while/body/eval_jaxpr/ppermute | solution.py:10
  360.8 13.6 %collective-permute-start = (bf16[32,5120]{1,0:T(8,128)(2,1)S(1)}, bf16[32,5120]{1,0:T(8,128)(2,1)S(1)}, u32[]{:S(2)}, u32[]{:S(2)}) collective-permute-start(bf16[32,5120]{1,0:T(8,128)(2,1)S(1)} %fusion.82), channel_id=1, source_target_pairs={{16,0},{32,16},{48,32},{64,48},{80,64},{96,80},{112,96},{128,112},... | collective-permute-start | bytes 983048 | tf_op jit(solution)/shard_map/while/body/eval_jaxpr/ppermute | solution.py:10
  374.5 4.4 copy-start.4
  381.3 13.6 %collective-permute-start.1 = (bf16[32,5120]{1,0:T(8,128)(2,1)S(1)}, bf16[32,5120]{1,0:T(8,128)(2,1)S(1)}, u32[]{:S(2)}, u32[]{:S(2)}) collective-permute-start(bf16[32,5120]{1,0:T(8,128)(2,1)S(1)} %fusion.83), channel_id=1, source_target_pairs={{0,16},{16,32},{32,48},{48,64},{64,80},{80,96},{96,112},{112,128},... | collective-permute-start | bytes 983048 | tf_op jit(solution)/shard_map/while/body/eval_jaxpr/ppermute | solution.py:10
  388.6 13.6 %collective-permute-start = (bf16[32,5120]{1,0:T(8,128)(2,1)S(1)}, bf16[32,5120]{1,0:T(8,128)(2,1)S(1)}, u32[]{:S(2)}, u32[]{:S(2)}) collective-permute-start(bf16[32,5120]{1,0:T(8,128)(2,1)S(1)} %fusion.82), channel_id=1, source_target_pairs={{16,0},{32,16},{48,32},{64,48},{80,64},{96,80},{112,96},{128,112},... | collective-permute-start | bytes 983048 | tf_op jit(solution)/shard_map/while/body/eval_jaxpr/ppermute | solution.py:10
  402.3 4.4 copy-start.4
  409.1 13.6 %collective-permute-start.1 = (bf16[32,5120]{1,0:T(8,128)(2,1)S(1)}, bf16[32,5120]{1,0:T(8,128)(2,1)S(1)}, u32[]{:S(2)}, u32[]{:S(2)}) collective-permute-start(bf16[32,5120]{1,0:T(8,128)(2,1)S(1)} %fusion.83), channel_id=1, source_target_pairs={{0,16},{16,32},{32,48},{48,64},{64,80},{80,96},{96,112},{112,128},... | collective-permute-start | bytes 983048 | tf_op jit(solution)/shard_map/while/body/eval_jaxpr/ppermute | solution.py:10
  416.4 13.6 %collective-permute-start = (bf16[32,5120]{1,0:T(8,128)(2,1)S(1)}, bf16[32,5120]{1,0:T(8,128)(2,1)S(1)}, u32[]{:S(2)}, u32[]{:S(2)}) collective-permute-start(bf16[32,5120]{1,0:T(8,128)(2,1)S(1)} %fusion.82), channel_id=1, source_target_pairs={{16,0},{32,16},{48,32},{64,48},{80,64},{96,80},{112,96},{128,112},... | collective-permute-start | bytes 983048 | tf_op jit(solution)/shard_map/while/body/eval_jaxpr/ppermute | solution.py:10
  430.1 4.4 copy-start.4
  437.0 13.6 %collective-permute-start.1 = (bf16[32,5120]{1,0:T(8,128)(2,1)S(1)}, bf16[32,5120]{1,0:T(8,128)(2,1)S(1)}, u32[]{:S(2)}, u32[]{:S(2)}) collective-permute-start(bf16[32,5120]{1,0:T(8,128)(2,1)S(1)} %fusion.83), channel_id=1, source_target_pairs={{0,16},{16,32},{32,48},{48,64},{64,80},{80,96},{96,112},{112,128},... | collective-permute-start | bytes 983048 | tf_op jit(solution)/shard_map/while/body/eval_jaxpr/ppermute | solution.py:10
  444.3 13.6 %collective-permute-start = (bf16[32,5120]{1,0:T(8,128)(2,1)S(1)}, bf16[32,5120]{1,0:T(8,128)(2,1)S(1)}, u32[]{:S(2)}, u32[]{:S(2)}) collective-permute-start(bf16[32,5120]{1,0:T(8,128)(2,1)S(1)} %fusion.82), channel_id=1, source_target_pairs={{16,0},{32,16},{48,32},{64,48},{80,64},{96,80},{112,96},{128,112},... | collective-permute-start | bytes 983048 | tf_op jit(solution)/shard_map/while/body/eval_jaxpr/ppermute | solution.py:10
  457.9 4.4 copy-start.4
  464.8 12.5 %collective-permute-start.1 = (bf16[32,5120]{1,0:T(8,128)(2,1)S(1)}, bf16[32,5120]{1,0:T(8,128)(2,1)S(1)}, u32[]{:S(2)}, u32[]{:S(2)}) collective-permute-start(bf16[32,5120]{1,0:T(8,128)(2,1)S(1)} %fusion.83), channel_id=1, source_target_pairs={{0,16},{16,32},{32,48},{48,64},{64,80},{80,96},{96,112},{112,128},... | collective-permute-start | bytes 983048 | tf_op jit(solution)/shard_map/while/body/eval_jaxpr/ppermute | solution.py:10
  472.1 12.6 %collective-permute-start = (bf16[32,5120]{1,0:T(8,128)(2,1)S(1)}, bf16[32,5120]{1,0:T(8,128)(2,1)S(1)}, u32[]{:S(2)}, u32[]{:S(2)}) collective-permute-start(bf16[32,5120]{1,0:T(8,128)(2,1)S(1)} %fusion.82), channel_id=1, source_target_pairs={{16,0},{32,16},{48,32},{64,48},{80,64},{96,80},{112,96},{128,112},... | collective-permute-start | bytes 983048 | tf_op jit(solution)/shard_map/while/body/eval_jaxpr/ppermute | solution.py:10
  484.7 4.4 copy-start.4
  491.6 11.7 %collective-permute-start.1 = (bf16[32,5120]{1,0:T(8,128)(2,1)S(1)}, bf16[32,5120]{1,0:T(8,128)(2,1)S(1)}, u32[]{:S(2)}, u32[]{:S(2)}) collective-permute-start(bf16[32,5120]{1,0:T(8,128)(2,1)S(1)} %fusion.83), channel_id=1, source_target_pairs={{0,16},{16,32},{32,48},{48,64},{64,80},{80,96},{96,112},{112,128},... | collective-permute-start | bytes 983048 | tf_op jit(solution)/shard_map/while/body/eval_jaxpr/ppermute | solution.py:10
  499.5 11.7 %collective-permute-start = (bf16[32,5120]{1,0:T(8,128)(2,1)S(1)}, bf16[32,5120]{1,0:T(8,128)(2,1)S(1)}, u32[]{:S(2)}, u32[]{:S(2)}) collective-permute-start(bf16[32,5120]{1,0:T(8,128)(2,1)S(1)} %fusion.82), channel_id=1, source_target_pairs={{16,0},{32,16},{48,32},{64,48},{80,64},{96,80},{112,96},{128,112},... | collective-permute-start | bytes 983048 | tf_op jit(solution)/shard_map/while/body/eval_jaxpr/ppermute | solution.py:10
  511.2 4.4 copy-start.4
  518.0 14.2 %collective-permute-start.1 = (bf16[32,5120]{1,0:T(8,128)(2,1)S(1)}, bf16[32,5120]{1,0:T(8,128)(2,1)S(1)}, u32[]{:S(2)}, u32[]{:S(2)}) collective-permute-start(bf16[32,5120]{1,0:T(8,128)(2,1)S(1)} %fusion.83), channel_id=1, source_target_pairs={{0,16},{16,32},{32,48},{48,64},{64,80},{80,96},{96,112},{112,128},... | collective-permute-start | bytes 983048 | tf_op jit(solution)/shard_map/while/body/eval_jaxpr/ppermute | solution.py:10
  528.5 11.7 %collective-permute-start = (bf16[32,5120]{1,0:T(8,128)(2,1)S(1)}, bf16[32,5120]{1,0:T(8,128)(2,1)S(1)}, u32[]{:S(2)}, u32[]{:S(2)}) collective-permute-start(bf16[32,5120]{1,0:T(8,128)(2,1)S(1)} %fusion.82), channel_id=1, source_target_pairs={{16,0},{32,16},{48,32},{64,48},{80,64},{96,80},{112,96},{128,112},... | collective-permute-start | bytes 983048 | tf_op jit(solution)/shard_map/while/body/eval_jaxpr/ppermute | solution.py:10
  540.2 4.4 copy-start.4
  547.1 14.2 %collective-permute-start.1 = (bf16[32,5120]{1,0:T(8,128)(2,1)S(1)}, bf16[32,5120]{1,0:T(8,128)(2,1)S(1)}, u32[]{:S(2)}, u32[]{:S(2)}) collective-permute-start(bf16[32,5120]{1,0:T(8,128)(2,1)S(1)} %fusion.83), channel_id=1, source_target_pairs={{0,16},{16,32},{32,48},{48,64},{64,80},{80,96},{96,112},{112,128},... | collective-permute-start | bytes 983048 | tf_op jit(solution)/shard_map/while/body/eval_jaxpr/ppermute | solution.py:10
  557.6 11.7 %collective-permute-start = (bf16[32,5120]{1,0:T(8,128)(2,1)S(1)}, bf16[32,5120]{1,0:T(8,128)(2,1)S(1)}, u32[]{:S(2)}, u32[]{:S(2)}) collective-permute-start(bf16[32,5120]{1,0:T(8,128)(2,1)S(1)} %fusion.82), channel_id=1, source_target_pairs={{16,0},{32,16},{48,32},{64,48},{80,64},{96,80},{112,96},{128,112},... | collective-permute-start | bytes 983048 | tf_op jit(solution)/shard_map/while/body/eval_jaxpr/ppermute | solution.py:10
  576.1 156.1 %reduce-scatter.15.cloned.1.call-start = ((), (), s32[]{:S(2)}) async-start(), calls=%async_computation.9 | async-start | bytes 2785280
  584.0 215.9 %reduce-scatter.9.cloned.1.call-start = ((), (), s32[]{:S(2)}) async-start(), calls=%async_computation.4 | async-start | bytes 2785280 | tf_op jit(solution)/shard_map/reduce_scatter | solution.py:119
  595.7 271.9 %reduce-scatter.11.cloned.1.call-start = ((), (), s32[]{:S(2)}) async-start(), calls=%async_computation.5 | async-start | bytes 2785280 | tf_op jit(solution)/shard_map/reduce_scatter | solution.py:125
  (13 other events, 53.3 us)
Sparse Core Ops, SparseCore 0:
  9.8 44.5 all-gather.6
  56.2 42.1 all-gather.4
  576.2 88.2 reduce-scatter.12
  666.9 65.2 reduce-scatter.14
  734.6 65.2 reduce-scatter.8
  802.3 65.2 reduce-scatter.10
where the time goes:
time: 878 us; the launch traced here: 876 us
  waiting for transfers between devices  539 us (61%)
  starting transfers between devices  147 us (17%)
  matrix products  110 us (13%)
  other arithmetic  40.5 us (5%)
  local copies, waits for them, and re-layouts  23.8 us (3%)
  between operations  14.2 us (2%)
    ppermute x34, waiting for transfers between devices, passed_along(): return lax.ppermute(block, axis, route)  191 us
    ppermute x34, starting transfers between devices, passed_along(): return lax.ppermute(block, axis, route)  147 us
    unnamed x8, waiting for transfers between devices  126 us
    reduce_scatter x1, waiting for transfers between devices, on_device(): lax.psum_scatter(out_up.astype(jnp.bfloat16), 'dp', scatter_dimension=0,...  67.7 us
    reduce_scatter x1, waiting for transfers between devices, on_device(): lax.psum_scatter(out_down.astype(jnp.bfloat16), 'dp', scatter_dimension=0...  65.4 us
    dot_general x34, matrix products, block_backward(): lax.dot_general(upstream, w_output, (((1,), (1,)), ((), ())), preferred_e...  62 us
    all_gather x1, waiting for transfers between devices, on_device(): lax.all_gather(w_in[0], 'dp', axis=1, tiled=True)  44.9 us
    all_gather x1, waiting for transfers between devices, on_device(): lax.all_gather(w_out[0], 'dp', axis=1, tiled=True)  44 us
  transfers between devices with their start and end apart: 40, of which 38 were waited for; matrix products, arithmetic and copies ran while one was open for 6% of the time, Pallas kernels for 0%

commit v1 on v0

v1 whole, which is shorter than its diff:
```python
import functools

import jax
import jax.numpy as jnp
from jax import lax
from jax.experimental import pallas as pl
from jax.experimental.pallas import tpu as pltpu
from jax.sharding import Mesh, PartitionSpec as P

SECTION = ("z", "xh")
CHIPS = ("xl", "y")
DP = ("xl", "y", "core")
PLANES = 8
SEQ = 32
SWAP = [(0, 1), (1, 0)]
BF, F32 = jnp.bfloat16, jnp.float32


def swap(block, axis):
    return lax.ppermute(block, axis, SWAP)


def dot(a, b, contract):
    return lax.dot_general(a, b, (contract, ((), ())), preferred_element_type=F32)


def time_scan(values, rates, reverse):
    rows = values.shape[0]
    place = lax.broadcasted_iota(jnp.int32, values.shape, 0) % SEQ
    for step in (1, 2, 4, 8, 16):
        if reverse:
            moved = pltpu.roll(values, rows - step, 0)
            inside = place < SEQ - step
        else:
            moved = pltpu.roll(values, step, 0)
            inside = place >= step
        values = values + jnp.where(inside, moved, 0.0) * jnp.exp(-rates * step)
    return values


def relay_kernel(mine, other, u_ref, m_ref, rates_ref, w_hbm, sg_ref, u1_ref, u2_ref, w_vmem, sems):
    copies = [
        pltpu.make_async_copy(w_hbm.at[i], w_vmem.at[i], sems.at[i]) for i in range(2)
    ]
    for copy in copies:
        copy.start()
    state = m_ref.shape[0]
    grad = mine[...] + other[...]
    first = time_scan(grad[:, :state], rates_ref[0:1, :], True).astype(BF)
    sg_ref[0] = first
    grad2 = grad[:, state:] + dot(first, m_ref[...], ((1,), (0,)))
    second = time_scan(grad2, rates_ref[1:2, :], True).astype(BF)
    sg_ref[1] = second
    width = u_ref.shape[1]
    tile = 512
    copies[0].wait()
    for at in range(0, width, tile):
        cols = pl.ds(at, tile)
        carried = dot(first, w_vmem[0, cols, :], ((1,), (1,)))
        u1_ref[:, cols] = (u_ref[:, cols].astype(F32) + carried).astype(BF)
    copies[1].wait()
    for at in range(0, width, tile):
        cols = pl.ds(at, tile)
        carried = dot(second, w_vmem[1, cols, :], ((1,), (1,)))
        u2_ref[:, cols] = (u1_ref[:, cols].astype(F32) + carried).astype(BF)


def relay_step(mine, other, upstream, between, rates, w_input):
    rows, width = upstream.shape
    state = between.shape[0]
    vmem = pl.BlockSpec(memory_space=pltpu.VMEM)
    return pl.pallas_call(
        relay_kernel,
        out_shape=(
            jax.ShapeDtypeStruct((2, rows, state), BF),
            jax.ShapeDtypeStruct((rows, width), BF),
            jax.ShapeDtypeStruct((rows, width), BF),
        ),
        in_specs=[vmem] * 5 + [pl.BlockSpec(memory_space=pl.ANY)],
        out_specs=(vmem, vmem, vmem),
        scratch_shapes=[
            pltpu.VMEM((2, width, state), BF),
            pltpu.SemaphoreType.DMA((2,)),
        ],
        compiler_params=pltpu.CompilerParams(vmem_limit_bytes=16 * 2**20),
        cost_estimate=pl.CostEstimate(
            flops=4 * rows * width * state, bytes_accessed=4 * width * state, transcendentals=0
        ),
    )(mine, other, upstream, between, rates, w_input)


def latent_kernel(mine, other, rates_ref, out_ref):
    for place in range(2):
        hidden = mine[place] + other[place]
        out_ref[place] = time_scan(hidden, rates_ref[place : place + 1, :], False).astype(BF)


def latents(mine, other, rates):
    vmem = pl.BlockSpec(memory_space=pltpu.VMEM)
    return pl.pallas_call(
        latent_kernel,
        out_shape=jax.ShapeDtypeStruct(mine.shape, BF),
        in_specs=[vmem] * 3,
        out_specs=vmem,
        compiler_params=pltpu.CompilerParams(vmem_limit_bytes=16 * 2**20),
    )(mine, other, rates)


def on_device(saved_a, saved_b, cot_a, cot_b, w_in, w_out, decay_rate):
    plane, half, core = lax.axis_index("z"), lax.axis_index("xh"), lax.axis_index("core")
    chips = lax.axis_size(CHIPS)
    micro, length, width = saved_a.shape[1:]
    part = width // (2 * chips)
    state = w_in.shape[3]

    def by_half(a, b):
        return jnp.where(half == 0, a, b)

    def by_core(a, b):
        return jnp.where(core == 0, a, b)

    def columns(block):
        even = jnp.concatenate(
            [block[..., 2 * i * part : (2 * i + 1) * part] for i in range(chips)], axis=-1
        )
        odd = jnp.concatenate(
            [block[..., (2 * i + 1) * part : (2 * i + 2) * part] for i in range(chips)], axis=-1
        )
        return by_core(even, odd), by_core(odd, even)

    def pair_rows(block, axis):
        keep, give = columns(block)
        got = swap(give, "core")
        return by_core(
            jnp.concatenate([keep, got], axis=axis), jnp.concatenate([got, keep], axis=axis)
        )

    def both_places(own_a, own_b):
        return jnp.stack([swap(by_half(own_b, own_a), "xh"), by_half(own_a, own_b)])

    shard_in = both_places(w_in[0, 0], w_in[0, 1])
    shard_out = pair_rows(both_places(w_out[0, 0], w_out[0, 1]), 1)
    rates = both_places(decay_rate[0, 0], decay_rate[0, 1])
    weights_out = lax.all_gather(shard_out, CHIPS, axis=1, tiled=True)
    weights_in = lax.all_gather(shard_in, CHIPS, axis=1, tiled=True)

    cot = pair_rows(by_half(cot_a, cot_b), 1)
    rows = cot.shape[1]
    inputs = pair_rows(both_places(saved_a[0], saved_b[0]), 2)

    between = dot(weights_in[0], weights_out[1], ((0,), (1,)))
    between = (between + swap(between, "core")).astype(BF)
    weights_out = weights_out.reshape(2 * state, width // 2)

    place = by_half(PLANES - 1 - plane, plane)
    uppers = jnp.zeros((micro + 1, 2, rows, width // 2), BF)
    states = jnp.zeros((micro + 1, 2, rows, state), BF)
    incoming = cot[0]
    steps = PLANES + micro - 1
    for step in range(steps):
        if 0 < step < micro:
            incoming = jnp.where(place == 0, cot[step], incoming)
        mine = dot(incoming, weights_out, ((1,), (1,)))
        state_grad, middle, passing = relay_step(
            mine, swap(mine, "core"), incoming, between, rates, weights_in
        )
        order = step - place
        slot = jnp.where((order >= 0) & (order < micro), order, micro)
        uppers = lax.dynamic_update_slice(uppers, incoming[None, None], (slot, 0, 0, 0))
        uppers = lax.dynamic_update_slice(uppers, middle[None, None], (slot, 1, 0, 0))
        states = lax.dynamic_update_slice(states, state_grad[None], (slot, 0, 0, 0))
        if step < steps - 1:
            route = []
            for at in range(PLANES - 1):
                if 0 <= step - at < micro:
                    route.append(((PLANES - 1 - at) * 2, (PLANES - 2 - at) * 2))
                    route.append((at * 2 + 1, (at + 1) * 2 + 1))
            incoming = lax.ppermute(passing, SECTION, route)

    def cut(block):
        return jnp.stack([block[..., i * part : (i + 1) * part] for i in range(chips)])

    def own_rows(block):
        return by_core(block[..., :length, :], block[..., length:, :])

    def all_rows(got):
        other = swap(got, "core")
        return by_core(
            jnp.concatenate([got, other], axis=-2), jnp.concatenate([other, got], axis=-2)
        )

    hidden = lax.dot_general(
        inputs.reshape(2, micro * rows, width // 2),
        weights_in,
        (((2,), (1,)), ((0,), (0,))),
        preferred_element_type=F32,
    )
    latent = latents(hidden, swap(hidden, "core"), rates).reshape(2, micro, rows, state)
    inputs_all = lax.all_to_all(cut(inputs), CHIPS, 0, 0)
    latent_own = own_rows(latent)
    latent_all = all_rows(
        lax.all_to_all(
            jnp.broadcast_to(latent_own[None], (chips,) + latent_own.shape), CHIPS, 0, 0
        )
    )

    states_own = own_rows(states[:micro])
    uppers_all = lax.all_to_all(cut(uppers[:micro]), CHIPS, 0, 0)
    states_all = all_rows(
        lax.all_to_all(
            jnp.broadcast_to(states_own[None], (chips,) + states_own.shape), CHIPS, 0, 0
        )
    )
    grad_in = jnp.stack(
        [
            dot(inputs_all[:, p], states_all[:, :, p], ((0, 1, 2), (0, 1, 2))).astype(BF)
            for p in range(2)
        ]
    )
    grad_out = jnp.stack(
        [
            dot(latent_all[:, p], uppers_all[:, :, p], ((0, 1, 2), (0, 1, 2))).astype(BF)
            for p in range(2)
        ]
    )
    pieces = grad_out.reshape(2, 2 * chips, state // (2 * chips), part).transpose(1, 0, 2, 3)
    pieces = lax.all_to_all(pieces, DP, 0, 0)
    grad_out = pieces.transpose(1, 2, 0, 3).reshape(2, state // (2 * chips), width)

    def home(both):
        other = swap(both[0], "xh").astype(F32)
        own = both[1].astype(F32)
        return jnp.stack([by_half(own, other), by_half(other, own)])[None]

    return home(grad_in), home(grad_out)


def solution(mesh):
    parts = Mesh(mesh.devices.reshape(PLANES, 2, 2, 4, 2), ("z", "xh", "xl", "y", "core"))
    rows = P(SECTION, None, DP, None)
    return jax.shard_map(
        on_device,
        mesh=parts,
        in_specs=(
            rows,
            rows,
            P(None, DP, None),
            P(None, DP, None),
            rows,
            rows,
            P(SECTION, None, None),
        ),
        out_specs=(rows, rows),
        check_vma=False,
    )
```

time: 878 us -> 360 us (0.41)
  waiting for transfers between devices: 539 us -> 148 us
  matrix products: 110 us -> 19.1 us
  starting transfers between devices: 147 us -> 110 us
  other arithmetic: 40.5 us -> 27.9 us
  local copies, waits for them, and re-layouts: 23.8 us -> 36.3 us
    ppermute x34 -> x30, waiting for transfers between devices: 191 us -> 55.6 us  [the longest x22 41.5 us: swap(): return lax.ppermute(block, axis, SWAP)]
    reduce_scatter x2 -> x0, waiting for transfers between devices: 133 us -> none  [the longest x1 67.7 us: on_device(): lax.psum_scatter(out_up.astype(jnp.bfloat16), 'dp', scatter_dimension=0,...]
    unnamed x8 -> x2, waiting for transfers between devices: 126 us -> 0.03 us
    dot_general x76 -> x15, matrix products: 110 us -> 19.1 us  [the longest x14 18.6 us: dot(): lax.dot_general(a, b, (contract, ((), ())), preferred_element_type=F32)]
    ppermute x34 -> x30, starting transfers between devices: 147 us -> 89.1 us  [the longest x22 75.9 us: swap(): return lax.ppermute(block, axis, SWAP)]
    all_to_all x0 -> x5, waiting for transfers between devices: none -> 37.1 us  [the longest x1 15.5 us: on_device(): inputs_all = lax.all_to_all(cut(inputs), CHIPS, 0, 0)]
    all_gather x2, waiting for transfers between devices: 88.9 us -> 55.6 us  [the longest x1 45.8 us: on_device(): weights_out = lax.all_gather(shard_out, CHIPS, axis=1, tiled=True)]
    dynamic_update_slice x51 -> x1, other arithmetic: 26.6 us -> 0.84 us  [on_device(): lax.dynamic_update_slice(uppers, incoming[None, None], (slot, 0, 0, 0))]
  transfers between devices with their start and end apart: 40 -> 37, of which waited for: 38 -> 21; matrix products, arithmetic and copies ran while one was open for 6% -> 19% of each run, Pallas kernels for 0% -> 0%
where the time goes in v1:
time: 360 us; the launch traced here: 357 us
  waiting for transfers between devices  148 us (41%)
  starting transfers between devices  110 us (31%)
  local copies, waits for them, and re-layouts  36.3 us (10%)
  other arithmetic  27.9 us (8%)
  matrix products  19.1 us (5%)
  between operations  14.9 us (4%)
    ppermute x22, starting transfers between devices, swap(): return lax.ppermute(block, axis, SWAP)  75.9 us
    all_gather x1, waiting for transfers between devices, on_device(): weights_out = lax.all_gather(shard_out, CHIPS, axis=1, tiled=True)  45.8 us
    ppermute x22, waiting for transfers between devices, swap(): return lax.ppermute(block, axis, SWAP)  41.5 us
    dot_general x14, matrix products, dot(): lax.dot_general(a, b, (contract, ((), ())), preferred_element_type=F32)  18.6 us
    pallas_call x9, other arithmetic, relay_step(): pl.pallas_call(relay_kernel, out_shape=(jax.ShapeDtypeStruct((2, rows, st...  17.3 us
    unnamed x44, local copies, waits for them, and re-layouts  16.8 us
    all_to_all x1, waiting for transfers between devices, on_device(): inputs_all = lax.all_to_all(cut(inputs), CHIPS, 0, 0)  15.5 us
    all_to_all x1, waiting for transfers between devices, on_device(): uppers_all = lax.all_to_all(cut(uppers[:micro]), CHIPS, 0, 0)  15.1 us
  transfers between devices with their start and end apart: 37, of which 21 were waited for; matrix products, arithmetic and copies ran while one was open for 19% of the time, Pallas kernels for 0%

profile of v1, /device:TPU:4, one launch (start us, length us, event | category | flops | bytes accessed | tf_op | source)
XLA Modules:
  0.0 357.0 jit_solution(6520216746786231702)
XLA Ops:
  7.2 1.0 select_bitcast_fusion.2
  8.2 2.3 collective-permute-start.6
  10.6 5.2 %collective-permute-done.6 = bf16[320,256]{1,0:T(8,128)(2,1)S(1)} collective-permute-done((bf16[320,256]{1,0:T(8,128)(2,1)S(1)}, bf16[320,256]{1,0:T(8,128)(2,1)S(1)}, u32[]{:S(2)}, u32[]{:S(2)}) %collective-permute-start.6) | collective-permute-done | bytes 163872 | tf_op jit(solution)/shard_map/ppermute | solution.py:20
  16.7 1.1 select_bitcast_fusion.3
  17.8 1.7 collective-permute-start.3
  19.5 5.2 %collective-permute-done.3 = bf16[16,5120]{1,0:T(8,128)(2,1)S(1)} collective-permute-done((bf16[16,5120]{1,0:T(8,128)(2,1)S(1)}, bf16[16,5120]{1,0:T(8,128)(2,1)S(1)}, u32[]{:S(2)}, u32[]{:S(2)}) %collective-permute-start.3) | collective-permute-done | bytes 163872 | tf_op jit(solution)/shard_map/ppermute | solution.py:20
  25.3 1.4 collective-permute-done.4
  28.5 1.7 collective-permute-start.8
  30.2 0.9 broadcast_select_fusion.1
  31.2 1.9 collective-permute-start
  34.4 1.2 maximum_select_fusion.3
  36.4 1.4 broadcast_in_dim.115
  38.6 23.9 %collective-permute-done = bf16[2,32,5120]{2,1,0:T(8,128)(2,1)S(1)} collective-permute-done((bf16[2,32,5120]{2,1,0:T(8,128)(2,1)}, bf16[2,32,5120]{2,1,0:T(8,128)(2,1)S(1)}, u32[]{:S(2)}, u32[]{:S(2)}) %collective-permute-start) | collective-permute-done | bytes 655392 | tf_op jit(solution)/shard_map/ppermute | solution.py:20
  62.6 1.2 concatenate.49
  64.1 1.2 concatenate.50
  65.2 9.8 %all-gather.5.cloned.1.call-done = bf16[2,2560,256]{2,1,0:T(8,128)(2,1)} async-done(((bf16[2,320,256]{2,1,0:T(8,128)(2,1)}), bf16[2,2560,256]{2,1,0:T(8,128)(2,1)}) %all-gather.5.cloned.1.call-update) | async-done | bytes 2621456 | tf_op jit(solution)/shard_map/all_gather | solution.py:145
  75.1 45.8 %all-gather.3.cloned.1.call-done = bf16[2,256,2560]{2,1,0:T(8,128)(2,1)} async-done(((bf16[2,32,2560]{2,1,0:T(8,128)(2,1)}), bf16[2,256,2560]{2,1,0:T(8,128)(2,1)}) %all-gather.3.cloned.1.call-update) | async-done | bytes 2621456 | tf_op jit(solution)/shard_map/all_gather | solution.py:144
  120.8 2.4 fusion
  123.4 0.9 fusion.60
  125.8 1.7 shard_map.95
  127.5 3.5 collective-permute-start.9
  131.3 7.2 %collective-permute-done.9 = bf16[64,2560]{1,0:T(8,128)(2,1)S(1)} collective-permute-done((bf16[64,2560]{1,0:T(8,128)(2,1)S(1)}, bf16[64,2560]{1,0:T(8,128)(2,1)S(1)}, u32[]{:S(2)}, u32[]{:S(2)}) %collective-permute-start.9) | collective-permute-done | bytes 327712 | tf_op jit(solution)/shard_map/ppermute | solution.py:178
  140.6 1.0 collective-permute-done.10
  141.6 1.7 shard_map.94
  143.3 4.6 %collective-permute-start.11 = (bf16[64,2560]{1,0:T(8,128)(2,1)S(1)}, bf16[64,2560]{1,0:T(8,128)(2,1)S(1)}, u32[]{:S(2)}, u32[]{:S(2)}) collective-permute-start(bf16[64,2560]{1,0:T(8,128)(2,1)S(1)} %get-tuple-element.76), channel_id=1, source_target_pairs={{224,192},{16,48},{192,160},{48,80},{225,193},{17,49},{193,161},{4... | collective-permute-start | bytes 983048 | tf_op jit(solution)/shard_map/ppermute | solution.py:178
  148.1 6.9 %collective-permute-done.11 = bf16[64,2560]{1,0:T(8,128)(2,1)S(1)} collective-permute-done((bf16[64,2560]{1,0:T(8,128)(2,1)S(1)}, bf16[64,2560]{1,0:T(8,128)(2,1)S(1)}, u32[]{:S(2)}, u32[]{:S(2)}) %collective-permute-start.11) | collective-permute-done | bytes 327712 | tf_op jit(solution)/shard_map/ppermute | solution.py:178
  155.0 0.9 fusion.101
  157.3 1.7 shard_map.93
  160.4 0.9 fusion.102
  162.8 2.2 shard_map.92
  165.0 1.4 collective-permute-start.15
  166.6 0.9 copy-done.7
  168.4 3.5 all-to-all-start.2
  171.9 2.8 fusion.103
  175.2 1.8 bitcast_dynamic-update-slice_fusion.9
  176.9 2.8 shard_map.91
  180.5 0.9 fusion.104
  182.8 1.7 shard_map.90
  187.6 1.7 shard_map.89
  192.4 1.7 shard_map.88
  194.1 0.9 collective-permute-start.23
  195.0 0.9 fusion.107
  197.4 2.2 shard_map.87
  199.6 1.6 fusion.20
  201.2 1.7 fusion.19
  202.9 1.6 fusion.18
  204.6 1.8 fusion.17
  206.4 1.6 fusion.16
  208.0 1.8 fusion.15
  210.6 5.4 %all-to-all-start.1 = ((bf16[8,2,2,32,256]{4,3,1,2,0:T(8,128)(2,1)}), bf16[8,2,2,32,256]{4,3,1,2,0:T(8,128)(2,1)S(1)}, u32[]{:S(2)}, u32[]{:S(2)}) async-start(bf16[8,2,2,32,256]{4,3,1,2,0:T(8,128)(2,1)} %broadcast_in_dim.112), calls=%async_computation.1 | async-start | bytes 1048576 | tf_op jit(solution)/shard_map/all_to_all | solution.py:210
  216.1 1.7 fusion.14
  217.8 1.7 fusion.13
  219.6 6.5 %all-to-all-done.1 = bf16[8,2,2,32,256]{4,3,1,2,0:T(8,128)(2,1)S(1)} async-done(((bf16[8,2,2,32,256]{4,3,1,2,0:T(8,128)(2,1)}), bf16[8,2,2,32,256]{4,3,1,2,0:T(8,128)(2,1)S(1)}, u32[]{:S(2)}, u32[]{:S(2)}) %all-to-all-start.1) | async-done | bytes 524320 | tf_op jit(solution)/shard_map/all_to_all | solution.py:210
  226.0 4.3 %all-to-all-start.3 = ((bf16[8,2,2,64,320]{4,3,1,2,0:T(8,128)(2,1)}), bf16[8,2,2,64,320]{4,3,1,2,0:T(8,128)(2,1)}, u32[]{:S(2)}, u32[]{:S(2)}) async-start(bf16[8,2,2,64,320]{4,3,1,2,0:T(8,128)(2,1)} %fusion.13), calls=%async_computation.3 | async-start | bytes 3145728 | tf_op jit(solution)/shard_map/all_to_all | solution.py:208
  235.0 15.1 %all-to-all-done.3 = bf16[8,2,2,64,320]{4,3,1,2,0:T(8,128)(2,1)} async-done(((bf16[8,2,2,64,320]{4,3,1,2,0:T(8,128)(2,1)}), bf16[8,2,2,64,320]{4,3,1,2,0:T(8,128)(2,1)}, u32[]{:S(2)}, u32[]{:S(2)}) %all-to-all-start.3) | async-done | bytes 1310752 | tf_op jit(solution)/shard_map/all_to_all | solution.py:208
  250.1 4.3 %all-to-all-start = ((bf16[8,2,2,64,320]{4,3,2,1,0:T(8,128)(2,1)}), bf16[8,2,2,64,320]{4,3,2,1,0:T(8,128)(2,1)}, u32[]{:S(2)}, u32[]{:S(2)}) async-start(bf16[8,2,2,64,320]{4,3,2,1,0:T(8,128)(2,1)} %fusion.21), calls=%async_computation | async-start | bytes 3145728 | tf_op jit(solution)/shard_map/all_to_all | solution.py:199
  255.1 1.6 fusion.3
  256.8 1.6 fusion.4
  259.4 15.5 %all-to-all-done = bf16[8,2,2,64,320]{4,3,2,1,0:T(8,128)(2,1)} async-done(((bf16[8,2,2,64,320]{4,3,2,1,0:T(8,128)(2,1)}), bf16[8,2,2,64,320]{4,3,2,1,0:T(8,128)(2,1)}, u32[]{:S(2)}, u32[]{:S(2)}) %all-to-all-start) | async-done | bytes 1310752 | tf_op jit(solution)/shard_map/all_to_all | solution.py:199
  274.9 3.7 %all-to-all-start.4 = ((bf16[16,2,16,320]{3,2,1,0:T(8,128)(2,1)}), bf16[16,2,16,320]{3,2,1,0:T(8,128)(2,1)S(1)}, u32[]{:S(2)}, u32[]{:S(2)}) async-start(bf16[16,2,16,320]{3,2,1,0:T(8,128)(2,1)} %copy.159), calls=%async_computation.4 | async-start | bytes 786432 | tf_op jit(solution)/shard_map/all_to_all | solution.py:227
  279.1 1.6 fusion.2
  280.6 56.8 %collective-permute-start.26 = (bf16[320,256]{1,0:T(8,128)(2,1)S(1)}, bf16[320,256]{1,0:T(8,128)(2,1)S(1)}, u32[]{:S(2)}, u32[]{:S(2)}) collective-permute-start(bf16[320,256]{1,0:T(8,128)(2,1)S(1)} %fusion.2), channel_id=1, source_target_pairs={{0,16},{16,0},{1,17},{17,1},{2,18},{18,2},{3,19},{19,3},{4,20},{20... | collective-permute-start | bytes 491528 | tf_op jit(solution)/shard_map/ppermute | solution.py:20
  337.8 8.0 %collective-permute-start.29 = (bf16[16,5120]{1,0:T(8,128)(2,1)S(1)}, bf16[16,5120]{1,0:T(8,128)(2,1)S(1)}, u32[]{:S(2)}, u32[]{:S(2)}) collective-permute-start(bf16[16,5120]{1,0:T(8,128)(2,1)S(1)} %squeeze.60), channel_id=1, source_target_pairs={{0,16},{16,0},{1,17},{17,1},{2,18},{18,2},{3,19},{19,3},{4,20},{20... | collective-permute-start | bytes 491528 | tf_op jit(solution)/shard_map/ppermute | solution.py:20
  345.7 1.5 fusion.8
  (152 shorter events, 37.1 us)
Async XLA Ops:
  7.2 67.9 %all-gather.5.cloned.1.call-start = ((), (), s32[]{:S(2)}) async-start(), calls=%async_computation.6 | async-start | bytes 2949120 | tf_op jit(solution)/shard_map/all_gather | solution.py:145
  8.2 7.5 %collective-permute-start.6 = (bf16[320,256]{1,0:T(8,128)(2,1)S(1)}, bf16[320,256]{1,0:T(8,128)(2,1)S(1)}, u32[]{:S(2)}, u32[]{:S(2)}) collective-permute-start(bf16[320,256]{1,0:T(8,128)(2,1)S(1)} %get-tuple-element.157), channel_id=1, source_target_pairs={{0,16},{16,0},{1,17},{17,1},{2,18},{18,2},{3,19},{19,3},{4,20},{20... | collective-permute-start | bytes 491528 | tf_op jit(solution)/shard_map/ppermute | solution.py:20
  16.6 10.9 %copy-start.9 = (bf16[2,32,5120]{2,1,0:T(8,128)(2,1)S(1)}, bf16[2,32,5120]{2,1,0:T(8,128)(2,1)}, u32[]{:S(2)}) copy-start(bf16[2,32,5120]{2,1,0:T(8,128)(2,1)} %param.9) | copy-start | bytes 1966084
  16.6 10.9 %copy-start.10 = (bf16[2,32,5120]{2,1,0:T(8,128)(2,1)S(1)}, bf16[2,32,5120]{2,1,0:T(8,128)(2,1)}, u32[]{:S(2)}) copy-start(bf16[2,32,5120]{2,1,0:T(8,128)(2,1)} %param.10) | copy-start | bytes 1966084
  16.6 104.2 %all-gather.3.cloned.1.call-start = ((), (), s32[]{:S(2)}) async-start(), calls=%async_computation.5 | async-start | bytes 2949120 | tf_op jit(solution)/shard_map/all_gather | solution.py:144
  17.8 6.9 %collective-permute-start.3 = (bf16[16,5120]{1,0:T(8,128)(2,1)S(1)}, bf16[16,5120]{1,0:T(8,128)(2,1)S(1)}, u32[]{:S(2)}, u32[]{:S(2)}) collective-permute-start(bf16[16,5120]{1,0:T(8,128)(2,1)S(1)} %get-tuple-element.178), channel_id=1, source_target_pairs={{0,16},{16,0},{1,17},{17,1},{2,18},{18,2},{3,19},{19,3},{4,20},{20... | collective-permute-start | bytes 491528 | tf_op jit(solution)/shard_map/ppermute | solution.py:20
  25.2 1.5 collective-permute-start.4
  27.6 0.9 copy-start.14
  27.6 2.6 copy-start.11
  27.6 2.6 copy-start.12
  28.3 5.4 %collective-permute-start.2 = (bf16[2,32,2560]{2,1,0:T(8,128)(2,1)S(1)}, bf16[2,32,2560]{2,1,0:T(8,128)(2,1)S(1)}, u32[]{:S(2)}, u32[]{:S(2)}) collective-permute-start(bf16[2,32,2560]{2,1,0:T(8,128)(2,1)S(1)} %get-tuple-element.134), channel_id=1, source_target_pairs={{0,1},{1,0},{2,3},{3,2},{4,5},{5,4},{6,7},{7,6},{8,9},{9,8},{10,11... | collective-permute-start | bytes 983048 | tf_op jit(solution)/shard_map/ppermute | solution.py:20
  28.5 5.2 %collective-permute-start.8 = (f32[256]{0:T(256)S(1)}, f32[256]{0:T(256)S(1)}, u32[]{:S(2)}, u32[]{:S(2)}) collective-permute-start(f32[256]{0:T(256)S(1)} %bitcast.311), channel_id=1, source_target_pairs={{0,16},{16,0},{1,17},{17,1},{2,18},{18,2},{3,19},{19,3},{4,20},{20... | collective-permute-start | bytes 3080 | tf_op jit(solution)/shard_map/ppermute | solution.py:20
  31.2 31.3 %collective-permute-start = (bf16[2,32,5120]{2,1,0:T(8,128)(2,1)}, bf16[2,32,5120]{2,1,0:T(8,128)(2,1)S(1)}, u32[]{:S(2)}, u32[]{:S(2)}) collective-permute-start(bf16[2,32,5120]{2,1,0:T(8,128)(2,1)} %get-tuple-element.130), channel_id=1, source_target_pairs={{0,16},{16,0},{1,17},{17,1},{2,18},{18,2},{3,19},{19,3},{4,20},{20... | collective-permute-start | bytes 1966088 | tf_op jit(solution)/shard_map/ppermute | solution.py:20
  33.7 0.7 copy-start.13
  120.8 2.5 copy-start.1
  123.2 2.6 copy-start
  123.2 2.6 copy-start.8
  123.2 1.6 collective-permute-start.7
  124.3 1.6 collective-permute-start.5
  124.9 6.1 %copy-start.5 = (bf16[2,2,32,2560]{3,2,1,0:T(8,128)(2,1)S(1)}, bf16[2,2,32,2560]{3,2,1,0:T(8,128)(2,1)}, u32[]{:S(2)}) copy-start(bf16[2,2,32,2560]{3,2,1,0:T(8,128)(2,1)} %concatenate.49) | copy-start | bytes 1966084
  124.9 6.1 %copy-start.6 = (bf16[2,2,32,2560]{3,2,1,0:T(8,128)(2,1)S(1)}, bf16[2,2,32,2560]{3,2,1,0:T(8,128)(2,1)}, u32[]{:S(2)}) copy-start(bf16[2,2,32,2560]{3,2,1,0:T(8,128)(2,1)} %concatenate.50) | copy-start | bytes 1966084
  127.5 11.0 %collective-permute-start.9 = (bf16[64,2560]{1,0:T(8,128)(2,1)S(1)}, bf16[64,2560]{1,0:T(8,128)(2,1)S(1)}, u32[]{:S(2)}, u32[]{:S(2)}) collective-permute-start(bf16[64,2560]{1,0:T(8,128)(2,1)S(1)} %get-tuple-element.70), channel_id=1, source_target_pairs={{224,192},{16,48},{225,193},{17,49},{226,194},{18,50},{227,195},{1... | collective-permute-start | bytes 983048 | tf_op jit(solution)/shard_map/ppermute | solution.py:178
  131.1 9.2 %collective-permute-start.1 = (bf16[2,2,32,2560]{3,2,1,0:T(8,128)(2,1)S(1)}, bf16[2,2,32,2560]{3,2,1,0:T(8,128)(2,1)S(1)}, u32[]{:S(2)}, u32[]{:S(2)}) collective-permute-start(bf16[2,2,32,2560]{3,2,1,0:T(8,128)(2,1)S(1)} %get-tuple-element.112), channel_id=1, source_target_pairs={{0,1},{1,0},{2,3},{3,2},{4,5},{5,4},{6,7},{7,6},{8,9},{9,8},{10,11... | collective-permute-start | bytes 1966088 | tf_op jit(solution)/shard_map/ppermute | solution.py:20
  140.2 1.4 collective-permute-start.10
  140.6 25.8 %copy-start.3 = (bf16[2,2,64,2560]{3,2,1,0:T(8,128)(2,1)}, bf16[2,2,64,2560]{3,2,1,0:T(8,128)(2,1)S(1)}, u32[]{:S(2)}) copy-start(bf16[2,2,64,2560]{3,2,1,0:T(8,128)(2,1)S(1)} %maximum_select_fusion) | copy-start | bytes 3932164
  143.3 11.6 %collective-permute-start.11 = (bf16[64,2560]{1,0:T(8,128)(2,1)S(1)}, bf16[64,2560]{1,0:T(8,128)(2,1)S(1)}, u32[]{:S(2)}, u32[]{:S(2)}) collective-permute-start(bf16[64,2560]{1,0:T(8,128)(2,1)S(1)} %get-tuple-element.76), channel_id=1, source_target_pairs={{224,192},{16,48},{192,160},{48,80},{225,193},{17,49},{193,161},{4... | collective-permute-start | bytes 983048 | tf_op jit(solution)/shard_map/ppermute | solution.py:178
  155.9 1.4 collective-permute-start.12
  159.0 1.4 collective-permute-start.13
  160.2 6.2 %collective-permute-start.27 = (f32[2,128,256]{2,1,0:T(8,128)S(1)}, f32[2,128,256]{2,1,0:T(8,128)S(1)}, u32[]{:S(2)}, u32[]{:S(2)}) collective-permute-start(f32[2,128,256]{2,1,0:T(8,128)S(1)} %fusion.108.mine), channel_id=1, source_target_pairs={{0,1},{1,0},{2,3},{3,2},{4,5},{5,4},{6,7},{7,6},{8,9},{9,8},{10,11... | collective-permute-start | bytes 786440 | tf_op jit(solution)/shard_map/ppermute | solution.py:20
  161.3 1.4 collective-permute-start.14
  165.0 7.0 %collective-permute-start.15 = (bf16[64,2560]{1,0:T(8,128)(2,1)}, bf16[64,2560]{1,0:T(8,128)(2,1)}, u32[]{:S(2)}, u32[]{:S(2)}) collective-permute-start(bf16[64,2560]{1,0:T(8,128)(2,1)} %get-tuple-element.58), channel_id=1, source_target_pairs={{160,128},{80,112},{128,96},{112,144},{161,129},{81,113},{129,97},... | collective-permute-start | bytes 983048 | tf_op jit(solution)/shard_map/ppermute | solution.py:178
  166.4 1.2 copy-start.7
  168.4 41.3 %all-to-all-start.2 = ((bf16[8,2,2,32,256]{4,3,1,2,0:T(8,128)(2,1)}), bf16[8,2,2,32,256]{4,3,1,2,0:T(8,128)(2,1)S(1)}, u32[]{:S(2)}, u32[]{:S(2)}) async-start(bf16[8,2,2,32,256]{4,3,1,2,0:T(8,128)(2,1)} %broadcast_in_dim.114), calls=%async_computation.2 | async-start | bytes 1048576 | tf_op jit(solution)/shard_map/all_to_all | solution.py:202
  174.7 2.2 collective-permute-start.16
  176.9 3.6 %copy-start.2 = (bf16[2,256,2560]{2,1,0:T(8,128)(2,1)S(1)}, bf16[2,256,2560]{2,1,0:T(8,128)(2,1)}, u32[]{:S(2)}) copy-start(bf16[2,256,2560]{2,1,0:T(8,128)(2,1)} %all-gather.3.cloned.1.call-done) | copy-start | bytes 7864324
  179.7 0.8 collective-permute-start.17
  181.4 1.4 collective-permute-start.18
  184.5 0.7 collective-permute-start.19
  186.2 1.4 collective-permute-start.20
  189.3 0.7 collective-permute-start.21
  191.0 1.4 collective-permute-start.22
  194.1 1.0 collective-permute-start.23
  195.9 1.4 collective-permute-start.24
  210.6 15.4 %all-to-all-start.1 = ((bf16[8,2,2,32,256]{4,3,1,2,0:T(8,128)(2,1)}), bf16[8,2,2,32,256]{4,3,1,2,0:T(8,128)(2,1)S(1)}, u32[]{:S(2)}, u32[]{:S(2)}) async-start(bf16[8,2,2,32,256]{4,3,1,2,0:T(8,128)(2,1)} %broadcast_in_dim.112), calls=%async_computation.1 | async-start | bytes 1048576 | tf_op jit(solution)/shard_map/all_to_all | solution.py:210
  216.1 14.2 %copy-start.4 = (bf16[2,2,64,2560]{3,2,1,0:T(8,128)(2,1)S(1)}, bf16[2,2,64,2560]{3,2,1,0:T(8,128)(2,1)}, u32[]{:S(2)}) copy-start(bf16[2,2,64,2560]{3,2,1,0:T(8,128)(2,1)} %copy-done.3) | copy-start | bytes 3932164
  226.0 24.1 %all-to-all-start.3 = ((bf16[8,2,2,64,320]{4,3,1,2,0:T(8,128)(2,1)}), bf16[8,2,2,64,320]{4,3,1,2,0:T(8,128)(2,1)}, u32[]{:S(2)}, u32[]{:S(2)}) async-start(bf16[8,2,2,64,320]{4,3,1,2,0:T(8,128)(2,1)} %fusion.13), calls=%async_computation.3 | async-start | bytes 3145728 | tf_op jit(solution)/shard_map/all_to_all | solution.py:208
  232.7 21.8 %collective-permute-start.28 = (bf16[8,2,2,32,256]{4,3,1,0,2:T(8,128)(2,1)}, bf16[8,2,2,32,256]{4,3,1,0,2:T(8,128)(2,1)S(1)}, u32[]{:S(2)}, u32[]{:S(2)}) collective-permute-start(bf16[8,2,2,32,256]{4,3,1,0,2:T(8,128)(2,1)} %copy.133), channel_id=1, source_target_pairs={{0,1},{1,0},{2,3},{3,2},{4,5},{5,4},{6,7},{7,6},{8,9},{9,8},{10,11... | collective-permute-start | bytes 1572872 | tf_op jit(solution)/shard_map/ppermute | solution.py:20
  250.1 24.8 %all-to-all-start = ((bf16[8,2,2,64,320]{4,3,2,1,0:T(8,128)(2,1)}), bf16[8,2,2,64,320]{4,3,2,1,0:T(8,128)(2,1)}, u32[]{:S(2)}, u32[]{:S(2)}) async-start(bf16[8,2,2,64,320]{4,3,2,1,0:T(8,128)(2,1)} %fusion.21), calls=%async_computation | async-start | bytes 3145728 | tf_op jit(solution)/shard_map/all_to_all | solution.py:199
  255.0 23.7 %collective-permute-start.25 = (bf16[8,2,2,32,256]{4,3,1,0,2:T(8,128)(2,1)S(1)}, bf16[8,2,2,32,256]{4,3,1,0,2:T(8,128)(2,1)S(1)}, u32[]{:S(2)}, u32[]{:S(2)}) collective-permute-start(bf16[8,2,2,32,256]{4,3,1,0,2:T(8,128)(2,1)S(1)} %copy.128), channel_id=1, source_target_pairs={{0,1},{1,0},{2,3},{3,2},{4,5},{5,4},{6,7},{7,6},{8,9},{9,8},{10,11... | collective-permute-start | bytes 1572872 | tf_op jit(solution)/shard_map/ppermute | solution.py:20
  274.9 62.5 %all-to-all-start.4 = ((bf16[16,2,16,320]{3,2,1,0:T(8,128)(2,1)}), bf16[16,2,16,320]{3,2,1,0:T(8,128)(2,1)S(1)}, u32[]{:S(2)}, u32[]{:S(2)}) async-start(bf16[16,2,16,320]{3,2,1,0:T(8,128)(2,1)} %copy.159), calls=%async_computation.4 | async-start | bytes 786432 | tf_op jit(solution)/shard_map/all_to_all | solution.py:227
  280.6 65.1 %collective-permute-start.26 = (bf16[320,256]{1,0:T(8,128)(2,1)S(1)}, bf16[320,256]{1,0:T(8,128)(2,1)S(1)}, u32[]{:S(2)}, u32[]{:S(2)}) collective-permute-start(bf16[320,256]{1,0:T(8,128)(2,1)S(1)} %fusion.2), channel_id=1, source_target_pairs={{0,16},{16,0},{1,17},{17,1},{2,18},{18,2},{3,19},{19,3},{4,20},{20... | collective-permute-start | bytes 491528 | tf_op jit(solution)/shard_map/ppermute | solution.py:20
  337.8 11.5 %collective-permute-start.29 = (bf16[16,5120]{1,0:T(8,128)(2,1)S(1)}, bf16[16,5120]{1,0:T(8,128)(2,1)S(1)}, u32[]{:S(2)}, u32[]{:S(2)}) collective-permute-start(bf16[16,5120]{1,0:T(8,128)(2,1)S(1)} %squeeze.60), channel_id=1, source_target_pairs={{0,16},{16,0},{1,17},{17,1},{2,18},{18,2},{3,19},{19,3},{4,20},{20... | collective-permute-start | bytes 491528 | tf_op jit(solution)/shard_map/ppermute | solution.py:20
Sparse Core Ops, SparseCore 0:
  16.7 58.3 all-gather.4
  76.8 43.9 all-gather.2
